TPU v7x, 32 devices: a whole 2x2x4 slice. The times are simulated.
32 devices in a mesh: view: 2 (over core), sky: 16 (over z, y, x).
Axes of the slice: x: 2, y: 2, z: 4, core: 2. Of those that a mesh axis runs over, the one named last changes fastest.
Arguments:
- pixels: bfloat16 [2, 32768, 128], P('view', 'sky'), may hold values from -6 to 6
- cotangent: bfloat16 [2, 32768, 128], P('view', 'sky'), may hold values from -6 to 6
- filters: bfloat16 [4, 128, 128], replicated, may hold values from -0.25 to 0.25
- lap_tiles: bfloat16 [16, 24, 256, 256], P('sky'), may hold values from -0.15625 to 0.15625
- tile_target: int32 [16, 24], P('sky'), may hold values from 0 to 7
- tile_source: int32 [16, 24], P('sky'), may hold values from 0 to 15
- tile_count: int32 [16], P('sky'), may hold values from 12 to 24, as said below
- send_blocks: int32 [16, 4, 2], P('sky'), may hold values from 0 to 7
Outputs:
- outputs: bfloat16 [2, 32768, 128], P('view', 'sky')
- pixel_grad: bfloat16 [2, 32768, 128], P('view', 'sky')
- filter_grad: float32 [4, 128, 128], replicated
Inputs may be any that keep to these rules, and one draw needn't show every extreme that they name: `tile_count`: every device has at least half of 24 live tiles, and some device has exactly 24. `tile_source`: indices below 8 are own blocks, the others received ones.
All inputs are finite; a program needn't handle non-finite values.
Results may differ from a plain program's by a relative error of at most 0.017.
Values may be sent and summed in bfloat16 or wider, within the bound.
A program may use at most 64 MiB of HBM per device.

v0:
```python
import math

import jax
import jax.numpy as jnp
from jax import lax
from jax.sharding import PartitionSpec as P

OFFSETS = (1, -1, 2, -2)


def passed_along(array, axis, by):
    size = lax.axis_size(axis)
    pairs = [(i, i + by) for i in range(size) if 0 <= i + by < size]
    return lax.ppermute(array, axis, pairs)


def spread_forward(pieces):
    return [passed_along(portion, "sky", offset) for offset, portion in zip(OFFSETS, pieces)]


def spread_backward(pieces):
    return [passed_along(portion, "sky", -offset) for offset, portion in zip(OFFSETS, pieces)]


def tile_products(values, tile_set, target, source, live_count, out_count, transposed):
    contraction = "tpq,tpc->tqc" if transposed else "tpq,tqc->tpc"
    picked = values[target] if transposed else values[source]
    routed = source if transposed else target
    products = jnp.einsum(contraction, tile_set, picked, preferred_element_type=jnp.float32)
    live_mask = jnp.arange(routed.shape[0]) < live_count
    routing = ((routed[None, :] == jnp.arange(out_count)[:, None]) & live_mask[None, :]).astype(
        jnp.float32
    )
    return jnp.einsum("bt,tpc->bpc", routing, products)


def per_device(
    pixels, cotangent, filters, lap_tiles, tile_target, tile_source, tile_count, send_blocks
):
    block_size = lap_tiles.shape[2]
    channels = pixels.shape[2]
    row_count = pixels.shape[1]
    block_count = row_count // block_size
    send_count = send_blocks.shape[2]
    ext_count = block_count + 4 * send_count
    tile_set = lap_tiles[0]
    target = tile_target[0]
    source = tile_source[0]
    live_count = tile_count[0]
    chosen = send_blocks[0]

    def forward_pieces(blocks):
        return [blocks[chosen[number]] for number in range(4)]

    def forward_finish(blocks, arrived):
        extended = jnp.concatenate([blocks] + arrived, axis=0)
        return tile_products(extended, tile_set, target, source, live_count, block_count, False)

    def transposed_start(blocks):
        slot_sums = tile_products(blocks, tile_set, target, source, live_count, ext_count, True)
        pieces = [
            slot_sums[block_count + number * send_count : block_count + (number + 1) * send_count]
            for number in range(4)
        ]
        return (slot_sums, pieces)

    def transposed_finish(slot_sums, arrived):
        combined = slot_sums[:block_count]
        for number in range(4):
            routing = (chosen[number][None, :] == jnp.arange(block_count)[:, None]).astype(
                jnp.float32
            )
            combined = combined + jnp.einsum("bj,jqc->bqc", routing, arrived[number])
        return combined

    def apply_forward(blocks):
        return forward_finish(blocks, spread_forward(forward_pieces(blocks)))

    def apply_transposed(blocks):
        slot_sums, pieces = transposed_start(blocks)
        return transposed_finish(slot_sums, spread_backward(pieces))

    upstream = cotangent[0]

    def filter_term(member):
        return jnp.einsum("pc,pd->cd", member, upstream, preferred_element_type=jnp.float32)

    base = pixels[0].reshape(block_count, block_size, channels)
    pulled = [
        jnp.einsum(
            "pd,cd->pc", upstream, filters[order], preferred_element_type=jnp.float32
        ).reshape(block_count, block_size, channels)
        for order in range(4)
    ]
    adj_three = pulled[3]
    grad_terms = [filter_term(pixels[0])]
    cheb_one = apply_forward(base).astype(jnp.bfloat16)
    grad_terms.append(filter_term(cheb_one.reshape(row_count, channels)))
    cheb_two = (2.0 * apply_forward(cheb_one) - base.astype(jnp.float32)).astype(jnp.bfloat16)
    grad_terms.append(filter_term(cheb_two.reshape(row_count, channels)))
    cheb_three = (2.0 * apply_forward(cheb_two) - cheb_one.astype(jnp.float32)).astype(jnp.bfloat16)
    grad_terms.append(filter_term(cheb_three.reshape(row_count, channels)))
    adj_two = pulled[2] + 2.0 * apply_transposed(adj_three.astype(jnp.bfloat16))
    adj_one = pulled[1] + 2.0 * apply_transposed(adj_two.astype(jnp.bfloat16)) - adj_three
    adj_zero = pulled[0] + apply_transposed(adj_one.astype(jnp.bfloat16)) - adj_two
    flattened = [
        member.reshape(row_count, channels) for member in (base, cheb_one, cheb_two, cheb_three)
    ]
    result = jnp.dot(flattened[0], filters[0], preferred_element_type=jnp.float32)
    for order in range(1, 4):
        result = result + jnp.dot(
            flattened[order], filters[order], preferred_element_type=jnp.float32
        )
    outputs = result.astype(jnp.bfloat16).reshape(1, row_count, channels)
    pixel_grad = adj_zero.astype(jnp.bfloat16).reshape(1, row_count, channels)
    stacked = lax.psum(jnp.stack(grad_terms), ("view", "sky"))
    scale = 1.0 / math.sqrt(lax.axis_size("view") * lax.axis_size("sky") * row_count)
    return (outputs, pixel_grad, stacked * scale)


def solution(mesh):
    return jax.shard_map(
        per_device,
        mesh=mesh,
        in_specs=(
            P("view", "sky", None),
            P("view", "sky", None),
            P(),
            P("sky", None, None, None),
            P("sky", None),
            P("sky", None),
            P("sky"),
            P("sky", None, None),
        ),
        out_specs=(P("view", "sky", None), P("view", "sky", None), P()),
        check_vma=False,
    )
```

profile of v0, /device:TPU:1, one launch (start us, length us, event | category | flops | bytes accessed | tf_op | source)
XLA Modules:
  0.0 390.2 jit_solution(17746026222789305608)
XLA Ops:
  13.6 3.3 fusion.16
  24.6 4.6 %collective-permute-start.15 = (bf16[2,256,128]{2,0,1:T(2,128)(2,1)}, bf16[2,256,128]{2,0,1:T(2,128)(2,1)}, u32[]{:S(2)}, u32[]{:S(2)}) collective-permute-start(bf16[2,256,128]{2,0,1:T(2,128)(2,1)} %get-tuple-element.16), channel_id=1, source_target_pairs={{0,2},{1,3},{2,4},{3,5},{4,6},{5,7},{6,8},{7,9},{8,10},{9,11},{10,... | collective-permute-start | bytes 393224 | tf_op jit(solution)/shard_map/ppermute | solution.py:14
  30.5 3.8 collective-permute-start.13
  37.3 3.3 collective-permute-start
  59.9 4.9 %collective-permute-start.2 = (bf16[2,256,128]{2,1,0:T(8,128)(2,1)}, bf16[2,256,128]{2,1,0:T(8,128)(2,1)S(1)}, u32[]{:S(2)}, u32[]{:S(2)}) collective-permute-start(bf16[2,256,128]{2,1,0:T(8,128)(2,1)} %gather_fusion.2), channel_id=1, source_target_pairs={{0,2},{1,3},{2,4},{3,5},{4,6},{5,7},{6,8},{7,9},{8,10},{9,11},{10,... | collective-permute-start | bytes 393224 | tf_op jit(solution)/shard_map/ppermute | solution.py:14
  73.0 3.3 gather_fusion.4
  76.2 3.8 fusion.22
  102.0 3.1 gather_fusion.16
  105.1 3.2 fusion.14
  114.1 5.0 %collective-permute-start.19 = (bf16[2,256,128]{2,0,1:T(2,128)(2,1)}, bf16[2,256,128]{2,0,1:T(2,128)(2,1)}, u32[]{:S(2)}, u32[]{:S(2)}) collective-permute-start(bf16[2,256,128]{2,0,1:T(2,128)(2,1)} %get-tuple-element.12), channel_id=1, source_target_pairs={{0,2},{1,3},{2,4},{3,5},{4,6},{5,7},{6,8},{7,9},{8,10},{9,11},{10,... | collective-permute-start | bytes 393224 | tf_op jit(solution)/shard_map/ppermute | solution.py:14
  123.6 5.5 %collective-permute-start.6 = (bf16[2,256,128]{2,0,1:T(2,128)(2,1)S(1)}, bf16[2,256,128]{2,0,1:T(2,128)(2,1)S(1)}, u32[]{:S(2)}, u32[]{:S(2)}) collective-permute-start(bf16[2,256,128]{2,0,1:T(2,128)(2,1)S(1)} %copy.20), channel_id=1, source_target_pairs={{0,2},{1,3},{2,4},{3,5},{4,6},{5,7},{6,8},{7,9},{8,10},{9,11},{10,... | collective-permute-start | bytes 393224 | tf_op jit(solution)/shard_map/ppermute | solution.py:14
  137.6 6.4 %concatenate.10 = bf16[16,256,128]{2,0,1:T(8,128)(2,1)} concatenate(bf16[8,256,128]{2,0,1:T(8,128)(2,1)} %copy-done.6, bf16[2,256,128]{2,0,1:T(2,128)(2,1)} %collective-permute-done.4, bf16[2,256,128]{2,0,1:T(2,128)(2,1)} %collective-permute-done.5, bf16[2,256,128]{2,0,1:T(2,128)(2,1)S(1)} %collective-permute-done.6, bf16[2,256,128]{2,0,1:T(2,128)(2,1)S(1)} %collective-permute-done.7), dimensions={0} | concatenate | bytes 2097152 | tf_op jit(solution)/shard_map/concatenate | solution.py:56
  146.5 3.3 gather_fusion.9
  149.8 3.8 fusion.20
  175.9 3.1 gather_fusion.17
  179.1 3.2 fusion.12
  188.7 6.4 %collective-permute-start.21 = (bf16[2,256,128]{2,0,1:T(2,128)(2,1)S(1)}, bf16[2,256,128]{2,0,1:T(2,128)(2,1)S(1)}, u32[]{:S(2)}, u32[]{:S(2)}) collective-permute-start(bf16[2,256,128]{2,0,1:T(2,128)(2,1)S(1)} %get-tuple-element.10), channel_id=1, source_target_pairs={{0,1},{1,2},{2,3},{3,4},{4,5},{5,6},{6,7},{7,8},{8,9},{9,10},{10,1... | collective-permute-start | bytes 393224 | tf_op jit(solution)/shard_map/ppermute | solution.py:14
  195.2 4.9 %collective-permute-start.23 = (bf16[2,256,128]{2,0,1:T(2,128)(2,1)S(1)}, bf16[2,256,128]{2,0,1:T(2,128)(2,1)S(1)}, u32[]{:S(2)}, u32[]{:S(2)}) collective-permute-start(bf16[2,256,128]{2,0,1:T(2,128)(2,1)S(1)} %get-tuple-element.8), channel_id=1, source_target_pairs={{0,2},{1,3},{2,4},{3,5},{4,6},{5,7},{6,8},{7,9},{8,10},{9,11},{10,... | collective-permute-start | bytes 393224 | tf_op jit(solution)/shard_map/ppermute | solution.py:14
  201.5 7.6 %collective-permute-start.10 = (bf16[2,256,128]{2,0,1:T(2,128)(2,1)S(1)}, bf16[2,256,128]{2,0,1:T(2,128)(2,1)}, u32[]{:S(2)}, u32[]{:S(2)}) collective-permute-start(bf16[2,256,128]{2,0,1:T(2,128)(2,1)S(1)} %copy.31), channel_id=1, source_target_pairs={{0,2},{1,3},{2,4},{3,5},{4,6},{5,7},{6,8},{7,9},{8,10},{9,11},{10,... | collective-permute-start | bytes 393224 | tf_op jit(solution)/shard_map/ppermute | solution.py:14
  220.0 3.4 collective-permute-done.9
  223.4 6.5 %concatenate.11 = bf16[16,256,128]{2,0,1:T(8,128)(2,1)} concatenate(bf16[8,256,128]{2,0,1:T(8,128)(2,1)} %copy-done.13, bf16[2,256,128]{2,0,1:T(2,128)(2,1)} %collective-permute-done.8, bf16[2,256,128]{2,0,1:T(2,128)(2,1)} %collective-permute-done.9, bf16[2,256,128]{2,0,1:T(2,128)(2,1)} %collective-permute-done.10, bf16[2,256,128]{2,0,1:T(2,128)(2,1)S(1)} %collective-permute-done.11), dimensions={0} | concatenate | bytes 2097152 | tf_op jit(solution)/shard_map/concatenate | solution.py:56
  232.4 3.3 gather_fusion.14
  235.7 3.7 fusion.18
  248.3 133.4 %all-reduce.2.cloned.1.call-done = f32[4,128,128]{2,1,0:T(8,128)} async-done(((f32[4,128,128]{2,1,0:T(8,128)}), f32[4,128,128]{2,1,0:T(8,128)}) %all-reduce.2.cloned.1.call-update) | async-done | bytes 262160 | tf_op jit(solution)/shard_map/psum | solution.py:116
  (205 shorter events, 141.8 us)
Async XLA Ops:
  7.2 374.5 %all-reduce.2.cloned.1.call-start = ((), (), s32[]{:S(2)}) async-start(), calls=%async_computation | async-start | bytes 524288 | tf_op jit(solution)/shard_map/psum | solution.py:116
  24.6 69.9 %collective-permute-start.15 = (bf16[2,256,128]{2,0,1:T(2,128)(2,1)}, bf16[2,256,128]{2,0,1:T(2,128)(2,1)}, u32[]{:S(2)}, u32[]{:S(2)}) collective-permute-start(bf16[2,256,128]{2,0,1:T(2,128)(2,1)} %get-tuple-element.16), channel_id=1, source_target_pairs={{0,2},{1,3},{2,4},{3,5},{4,6},{5,7},{6,8},{7,9},{8,10},{9,11},{10,... | collective-permute-start | bytes 393224 | tf_op jit(solution)/shard_map/ppermute | solution.py:14
  29.2 66.7 %collective-permute-start.14 = (bf16[2,256,128]{2,0,1:T(2,128)(2,1)}, bf16[2,256,128]{2,0,1:T(2,128)(2,1)}, u32[]{:S(2)}, u32[]{:S(2)}) collective-permute-start(bf16[2,256,128]{2,0,1:T(2,128)(2,1)} %get-tuple-element.17), channel_id=1, source_target_pairs={{2,0},{3,1},{4,2},{5,3},{6,4},{7,5},{8,6},{9,7},{10,8},{11,9},{12,... | collective-permute-start | bytes 393224 | tf_op jit(solution)/shard_map/ppermute | solution.py:14
  30.5 66.8 %collective-permute-start.13 = (bf16[2,256,128]{2,0,1:T(2,128)(2,1)}, bf16[2,256,128]{2,0,1:T(2,128)(2,1)}, u32[]{:S(2)}, u32[]{:S(2)}) collective-permute-start(bf16[2,256,128]{2,0,1:T(2,128)(2,1)} %get-tuple-element.18), channel_id=1, source_target_pairs={{0,1},{1,2},{2,3},{3,4},{4,5},{5,6},{6,7},{7,8},{8,9},{9,10},{10,1... | collective-permute-start | bytes 393224 | tf_op jit(solution)/shard_map/ppermute | solution.py:14
  37.3 22.5 %collective-permute-start = (bf16[2,256,128]{2,1,0:T(8,128)(2,1)}, bf16[2,256,128]{2,1,0:T(8,128)(2,1)S(1)}, u32[]{:S(2)}, u32[]{:S(2)}) collective-permute-start(bf16[2,256,128]{2,1,0:T(8,128)(2,1)} %gather_fusion), channel_id=1, source_target_pairs={{0,1},{1,2},{2,3},{3,4},{4,5},{5,6},{6,7},{7,8},{8,9},{9,10},{10,1... | collective-permute-start | bytes 393224 | tf_op jit(solution)/shard_map/ppermute | solution.py:14
  43.5 21.9 %collective-permute-start.1 = (bf16[2,256,128]{2,1,0:T(8,128)(2,1)}, bf16[2,256,128]{2,1,0:T(8,128)(2,1)S(1)}, u32[]{:S(2)}, u32[]{:S(2)}) collective-permute-start(bf16[2,256,128]{2,1,0:T(8,128)(2,1)} %gather_fusion.1), channel_id=1, source_target_pairs={{1,0},{2,1},{3,2},{4,3},{5,4},{6,5},{7,6},{8,7},{9,8},{10,9},{11,1... | collective-permute-start | bytes 393224 | tf_op jit(solution)/shard_map/ppermute | solution.py:14
  59.9 7.5 %collective-permute-start.2 = (bf16[2,256,128]{2,1,0:T(8,128)(2,1)}, bf16[2,256,128]{2,1,0:T(8,128)(2,1)S(1)}, u32[]{:S(2)}, u32[]{:S(2)}) collective-permute-start(bf16[2,256,128]{2,1,0:T(8,128)(2,1)} %gather_fusion.2), channel_id=1, source_target_pairs={{0,2},{1,3},{2,4},{3,5},{4,6},{5,7},{6,8},{7,9},{8,10},{9,11},{10,... | collective-permute-start | bytes 393224 | tf_op jit(solution)/shard_map/ppermute | solution.py:14
  65.4 6.8 %collective-permute-start.3 = (bf16[2,256,128]{2,1,0:T(8,128)(2,1)}, bf16[2,256,128]{2,1,0:T(8,128)(2,1)S(1)}, u32[]{:S(2)}, u32[]{:S(2)}) collective-permute-start(bf16[2,256,128]{2,1,0:T(8,128)(2,1)} %gather_fusion.3), channel_id=1, source_target_pairs={{2,0},{3,1},{4,2},{5,3},{6,4},{7,5},{8,6},{9,7},{10,8},{11,9},{12,... | collective-permute-start | bytes 393224 | tf_op jit(solution)/shard_map/ppermute | solution.py:14
  67.4 31.3 %collective-permute-start.12 = (bf16[2,256,128]{2,0,1:T(2,128)(2,1)}, bf16[2,256,128]{2,0,1:T(2,128)(2,1)}, u32[]{:S(2)}, u32[]{:S(2)}) collective-permute-start(bf16[2,256,128]{2,0,1:T(2,128)(2,1)} %get-tuple-element.15), channel_id=1, source_target_pairs={{1,0},{2,1},{3,2},{4,3},{5,4},{6,5},{7,6},{8,7},{9,8},{10,9},{11,1... | collective-permute-start | bytes 393224 | tf_op jit(solution)/shard_map/ppermute | solution.py:14
  114.1 54.2 %collective-permute-start.19 = (bf16[2,256,128]{2,0,1:T(2,128)(2,1)}, bf16[2,256,128]{2,0,1:T(2,128)(2,1)}, u32[]{:S(2)}, u32[]{:S(2)}) collective-permute-start(bf16[2,256,128]{2,0,1:T(2,128)(2,1)} %get-tuple-element.12), channel_id=1, source_target_pairs={{0,2},{1,3},{2,4},{3,5},{4,6},{5,7},{6,8},{7,9},{8,10},{9,11},{10,... | collective-permute-start | bytes 393224 | tf_op jit(solution)/shard_map/ppermute | solution.py:14
  119.3 13.5 %collective-permute-start.4 = (bf16[2,256,128]{2,0,1:T(2,128)(2,1)S(1)}, bf16[2,256,128]{2,0,1:T(2,128)(2,1)}, u32[]{:S(2)}, u32[]{:S(2)}) collective-permute-start(bf16[2,256,128]{2,0,1:T(2,128)(2,1)S(1)} %copy.16), channel_id=1, source_target_pairs={{0,1},{1,2},{2,3},{3,4},{4,5},{5,6},{6,7},{7,8},{8,9},{9,10},{10,1... | collective-permute-start | bytes 393224 | tf_op jit(solution)/shard_map/ppermute | solution.py:14
  121.8 12.3 %collective-permute-start.5 = (bf16[2,256,128]{2,0,1:T(2,128)(2,1)S(1)}, bf16[2,256,128]{2,0,1:T(2,128)(2,1)}, u32[]{:S(2)}, u32[]{:S(2)}) collective-permute-start(bf16[2,256,128]{2,0,1:T(2,128)(2,1)S(1)} %copy.18), channel_id=1, source_target_pairs={{1,0},{2,1},{3,2},{4,3},{5,4},{6,5},{7,6},{8,7},{9,8},{10,9},{11,1... | collective-permute-start | bytes 393224 | tf_op jit(solution)/shard_map/ppermute | solution.py:14
  123.6 12.7 %collective-permute-start.6 = (bf16[2,256,128]{2,0,1:T(2,128)(2,1)S(1)}, bf16[2,256,128]{2,0,1:T(2,128)(2,1)S(1)}, u32[]{:S(2)}, u32[]{:S(2)}) collective-permute-start(bf16[2,256,128]{2,0,1:T(2,128)(2,1)S(1)} %copy.20), channel_id=1, source_target_pairs={{0,2},{1,3},{2,4},{3,5},{4,6},{5,7},{6,8},{7,9},{8,10},{9,11},{10,... | collective-permute-start | bytes 393224 | tf_op jit(solution)/shard_map/ppermute | solution.py:14
  129.3 8.3 %collective-permute-start.7 = (bf16[2,256,128]{2,0,1:T(2,128)(2,1)S(1)}, bf16[2,256,128]{2,0,1:T(2,128)(2,1)S(1)}, u32[]{:S(2)}, u32[]{:S(2)}) collective-permute-start(bf16[2,256,128]{2,0,1:T(2,128)(2,1)S(1)} %copy.22), channel_id=1, source_target_pairs={{2,0},{3,1},{4,2},{5,3},{6,4},{7,5},{8,6},{9,7},{10,8},{11,9},{12,... | collective-permute-start | bytes 393224 | tf_op jit(solution)/shard_map/ppermute | solution.py:14
  132.8 37.0 %collective-permute-start.18 = (bf16[2,256,128]{2,0,1:T(2,128)(2,1)}, bf16[2,256,128]{2,0,1:T(2,128)(2,1)}, u32[]{:S(2)}, u32[]{:S(2)}) collective-permute-start(bf16[2,256,128]{2,0,1:T(2,128)(2,1)} %get-tuple-element.13), channel_id=1, source_target_pairs={{2,0},{3,1},{4,2},{5,3},{6,4},{7,5},{8,6},{9,7},{10,8},{11,9},{12,... | collective-permute-start | bytes 393224 | tf_op jit(solution)/shard_map/ppermute | solution.py:14
  134.1 37.1 %collective-permute-start.17 = (bf16[2,256,128]{2,0,1:T(2,128)(2,1)}, bf16[2,256,128]{2,0,1:T(2,128)(2,1)}, u32[]{:S(2)}, u32[]{:S(2)}) collective-permute-start(bf16[2,256,128]{2,0,1:T(2,128)(2,1)} %get-tuple-element.14), channel_id=1, source_target_pairs={{0,1},{1,2},{2,3},{3,4},{4,5},{5,6},{6,7},{7,8},{8,9},{9,10},{10,1... | collective-permute-start | bytes 393224 | tf_op jit(solution)/shard_map/ppermute | solution.py:14
  136.3 36.2 %collective-permute-start.16 = (bf16[2,256,128]{2,0,1:T(2,128)(2,1)}, bf16[2,256,128]{2,0,1:T(2,128)(2,1)}, u32[]{:S(2)}, u32[]{:S(2)}) collective-permute-start(bf16[2,256,128]{2,0,1:T(2,128)(2,1)} %get-tuple-element.11), channel_id=1, source_target_pairs={{1,0},{2,1},{3,2},{4,3},{5,4},{6,5},{7,6},{8,7},{9,8},{10,9},{11,1... | collective-permute-start | bytes 393224 | tf_op jit(solution)/shard_map/ppermute | solution.py:14
  187.3 24.0 %collective-permute-start.22 = (bf16[2,256,128]{2,0,1:T(2,128)(2,1)S(1)}, bf16[2,256,128]{2,0,1:T(2,128)(2,1)S(1)}, u32[]{:S(2)}, u32[]{:S(2)}) collective-permute-start(bf16[2,256,128]{2,0,1:T(2,128)(2,1)S(1)} %get-tuple-element.9), channel_id=1, source_target_pairs={{2,0},{3,1},{4,2},{5,3},{6,4},{7,5},{8,6},{9,7},{10,8},{11,9},{12,... | collective-permute-start | bytes 393224 | tf_op jit(solution)/shard_map/ppermute | solution.py:14
  188.7 24.5 %collective-permute-start.21 = (bf16[2,256,128]{2,0,1:T(2,128)(2,1)S(1)}, bf16[2,256,128]{2,0,1:T(2,128)(2,1)S(1)}, u32[]{:S(2)}, u32[]{:S(2)}) collective-permute-start(bf16[2,256,128]{2,0,1:T(2,128)(2,1)S(1)} %get-tuple-element.10), channel_id=1, source_target_pairs={{0,1},{1,2},{2,3},{3,4},{4,5},{5,6},{6,7},{7,8},{8,9},{9,10},{10,1... | collective-permute-start | bytes 393224 | tf_op jit(solution)/shard_map/ppermute | solution.py:14
  195.2 21.3 %collective-permute-start.23 = (bf16[2,256,128]{2,0,1:T(2,128)(2,1)S(1)}, bf16[2,256,128]{2,0,1:T(2,128)(2,1)S(1)}, u32[]{:S(2)}, u32[]{:S(2)}) collective-permute-start(bf16[2,256,128]{2,0,1:T(2,128)(2,1)S(1)} %get-tuple-element.8), channel_id=1, source_target_pairs={{0,2},{1,3},{2,4},{3,5},{4,6},{5,7},{6,8},{7,9},{8,10},{9,11},{10,... | collective-permute-start | bytes 393224 | tf_op jit(solution)/shard_map/ppermute | solution.py:14
  200.1 18.3 %collective-permute-start.20 = (bf16[2,256,128]{2,0,1:T(2,128)(2,1)S(1)}, bf16[2,256,128]{2,0,1:T(2,128)(2,1)S(1)}, u32[]{:S(2)}, u32[]{:S(2)}) collective-permute-start(bf16[2,256,128]{2,0,1:T(2,128)(2,1)S(1)} %get-tuple-element.7), channel_id=1, source_target_pairs={{1,0},{2,1},{3,2},{4,3},{5,4},{6,5},{7,6},{8,7},{9,8},{10,9},{11,1... | collective-permute-start | bytes 393224 | tf_op jit(solution)/shard_map/ppermute | solution.py:14
  201.5 18.5 %collective-permute-start.10 = (bf16[2,256,128]{2,0,1:T(2,128)(2,1)S(1)}, bf16[2,256,128]{2,0,1:T(2,128)(2,1)}, u32[]{:S(2)}, u32[]{:S(2)}) collective-permute-start(bf16[2,256,128]{2,0,1:T(2,128)(2,1)S(1)} %copy.31), channel_id=1, source_target_pairs={{0,2},{1,3},{2,4},{3,5},{4,6},{5,7},{6,8},{7,9},{8,10},{9,11},{10,... | collective-permute-start | bytes 393224 | tf_op jit(solution)/shard_map/ppermute | solution.py:14
  211.3 8.7 %collective-permute-start.11 = (bf16[2,256,128]{2,0,1:T(2,128)(2,1)S(1)}, bf16[2,256,128]{2,0,1:T(2,128)(2,1)S(1)}, u32[]{:S(2)}, u32[]{:S(2)}) collective-permute-start(bf16[2,256,128]{2,0,1:T(2,128)(2,1)S(1)} %copy.33), channel_id=1, source_target_pairs={{2,0},{3,1},{4,2},{5,3},{6,4},{7,5},{8,6},{9,7},{10,8},{11,9},{12,... | collective-permute-start | bytes 393224 | tf_op jit(solution)/shard_map/ppermute | solution.py:14
  216.5 7.0 %collective-permute-start.9 = (bf16[2,256,128]{2,0,1:T(2,128)(2,1)S(1)}, bf16[2,256,128]{2,0,1:T(2,128)(2,1)}, u32[]{:S(2)}, u32[]{:S(2)}) collective-permute-start(bf16[2,256,128]{2,0,1:T(2,128)(2,1)S(1)} %copy.29), channel_id=1, source_target_pairs={{1,0},{2,1},{3,2},{4,3},{5,4},{6,5},{7,6},{8,7},{9,8},{10,9},{11,1... | collective-permute-start | bytes 393224 | tf_op jit(solution)/shard_map/ppermute | solution.py:14
  (40 other events, 293.4 us)
Sparse Core Ops, SparseCore 0:
  245.9 135.6 all-reduce.1
where the time goes:
time: 395 us; the launch traced here: 390 us
  waiting for transfers between devices  140 us (35%)
  local copies, waits for them, and re-layouts  95.7 us (24%)
  starting transfers between devices  69.9 us (18%)
  matrix products  64.3 us (16%)
  between operations  15.5 us (4%)
  other arithmetic  5.03 us (1%)
    psum x1, waiting for transfers between devices, per_device(): stacked = lax.psum(jnp.stack(grad_terms), ('view', 'sky'))  133 us
    ppermute x24, starting transfers between devices, passed_along(): return lax.ppermute(array, axis, pairs)  69.8 us
    gather x20, local copies, waits for them, and re-layouts, forward_pieces(): return [blocks[chosen[number]] for number in range(4)]  26.8 us
    dot_general x6, matrix products, tile_products(): jnp.einsum(contraction, tile_set, picked, preferred_element_type=jnp.floa...  21 us
    gather x6, local copies, waits for them, and re-layouts, tile_products(): picked = values[target] if transposed else values[source]  19.1 us
    concatenate x5, local copies, waits for them, and re-layouts, forward_finish(): extended = jnp.concatenate([blocks] + arrived, axis=0)  18.5 us
    dot_general x6, local copies, waits for them, and re-layouts, tile_products(): jnp.einsum(contraction, tile_set, picked, preferred_element_type=jnp.floa...  16.5 us
    dot_general x12, matrix products, transposed_finish(): combined = combined + jnp.einsum('bj,jqc->bqc', routing, arrived[number])  15 us
  transfers between devices with their start and end apart: 25, of which 3 were waited for; matrix products, arithmetic and copies ran while one was open for 24% of the time, Pallas kernels for 0%

commit v1 on v0

v1 whole, which is shorter than its diff:
```python
import functools
import math

import jax
import jax.numpy as jnp
from jax import lax
from jax.experimental import pallas as pl
from jax.experimental.pallas import tpu as pltpu
from jax.sharding import PartitionSpec as P

OFFSETS = (1, -1, 2, -2)
MESH = pl.DeviceIdType.MESH
STRIDE = 64
BIG = 1 << 20
GROUP = 8


def radices_of(size):
    found = []
    while size > 1:
        step = 4 if size % 4 == 0 else (2 if size % 2 == 0 else size)
        found.append(step)
        size //= step
    return found


def smallest(values):
    while len(values) > 1:
        paired = [jnp.minimum(a, b) for a, b in zip(values[::2], values[1::2])]
        values = paired + (values[-1:] if len(values) % 2 else [])
    return values[0]


def order_slots(keys, key_count, perm, keep, last):
    codes = [key * STRIDE + number for number, key in enumerate(keys)]

    def pick(place, carry):
        before, before_key = carry
        code = smallest([jnp.where(c > before, c, BIG) for c in codes])
        key = lax.div(code, STRIDE)
        perm[place] = code - key * STRIDE
        keep[place] = jnp.where(key == before_key, 1.0, 0.0).astype(jnp.float32)
        return code, key

    lax.fori_loop(0, len(keys), pick, (jnp.int32(-1), jnp.int32(-1)))

    def ends(key, carry):
        upto = sum(jnp.where(c < (key + 1) * STRIDE, 1, 0) for c in codes)
        under = sum(jnp.where(c < key * STRIDE, 1, 0) for c in codes)
        last[key] = jnp.where(upto > under, upto, 0)
        return carry

    lax.fori_loop(0, key_count, ends, 0)


def kernel(
    sky_size, scale,
    pixels, cotangent, filters, target, source, live, chosen, tiles_hbm,
    outputs, pixel_grad, filter_grad,
    tiles, ext0, ext1, ext2, latest, out_f0, out_f1, out_f2, out_b0, out_b1, out_b2,
    in_b0, in_b1, in_b2, cot_t, u, adj_three, adj_two, adj_one, adj_zero,
    part_f, part_b, part_a, grads,
    red_send_a, red_land_a, red_out_a, red_slots_a, red_final_a,
    red_send_b, red_land_b, red_out_b, red_slots_b, red_final_b,
    perm_f, perm_b, perm_a, keep_f, keep_b, keep_a, last_f, last_b, last_a,
    tile_sem, f_send, f_recv, b_send, b_recv, r_send, r_recv,
):
    me = lax.axis_index("sky")
    view = lax.axis_index("view")
    blocks, size, channels = pixels.shape
    max_tiles = tiles.shape[0]
    ext_count = ext0.shape[0]
    sends = (ext_count - blocks) // len(OFFSETS)
    radices = radices_of(sky_size)
    exts, outs_f = (ext0, ext1, ext2), (out_f0, out_f1, out_f2)
    outs_b, ins_b = (out_b0, out_b1, out_b2), (in_b0, in_b1, in_b2)

    tile_copy = pltpu.make_async_copy(tiles_hbm, tiles, tile_sem)
    tile_copy.start()

    def inside(place):
        return jnp.logical_and(place >= 0, place < sky_size)

    groups = []
    below = 1
    for radix in radices:
        spot = lax.rem(lax.div(me, below), radix)
        groups.append((below, radix, spot))
        below *= radix

    def partner(group, shift):
        below, radix, spot = group
        return me + (lax.rem(spot + shift, radix) - spot) * below

    barrier = pltpu.get_barrier_semaphore()
    peers = 1
    for offset in OFFSETS:
        peers = peers + jnp.where(inside(me + offset), 1, 0)
        @pl.when(inside(me + offset))
        def _():
            pl.semaphore_signal(barrier, inc=1, device_id={"sky": me + offset}, device_id_type=MESH)
    for group in groups:
        for shift in range(1, group[1]):
            other = partner(group, shift)
            far = (other - me) * (other - me) > 4
            peers = peers + jnp.where(far, 1, 0)
            @pl.when(far)
            def _():
                pl.semaphore_signal(barrier, inc=1, device_id={"sky": other}, device_id_type=MESH)
    pl.semaphore_signal(barrier, inc=1, device_id={"view": 1 - view}, device_id_type=MESH)

    for number, offset in enumerate(OFFSETS):
        at = pl.ds(blocks + number * sends, sends)
        @pl.when(jnp.logical_not(inside(me - offset)))
        def _():
            for ext in exts:
                ext[at] = jnp.zeros((sends, size, channels), jnp.bfloat16)

        @pl.when(jnp.logical_not(inside(me + offset)))
        def _():
            for landed in ins_b:
                landed[pl.ds(number * sends, sends)] = jnp.zeros(
                    (sends, channels, size), jnp.bfloat16
                )

    def stage_forward(step, blocks_ref):
        for slot in range(len(OFFSETS) * sends):
            outs_f[step][slot] = blocks_ref[chosen[slot]]

    def copy_forward(step, number):
        return pltpu.make_async_remote_copy(
            src_ref=outs_f[step].at[pl.ds(number * sends, sends)],
            dst_ref=exts[step].at[pl.ds(blocks + number * sends, sends)],
            send_sem=f_send.at[step, number],
            recv_sem=f_recv.at[step, number],
            device_id={"sky": me + OFFSETS[number]},
            device_id_type=MESH,
        )

    def copy_backward(step, number):
        return pltpu.make_async_remote_copy(
            src_ref=outs_b[step].at[pl.ds(number * sends, sends)],
            dst_ref=ins_b[step].at[pl.ds(number * sends, sends)],
            send_sem=b_send.at[step, number],
            recv_sem=b_recv.at[step, number],
            device_id={"sky": me - OFFSETS[number]},
            device_id_type=MESH,
        )

    def start_all(copy, step, sign):
        for number in (3, 2, 1, 0):
            @pl.when(inside(me + sign * OFFSETS[number]))
            def _():
                copy(step, number).start()

    def wait_arrivals(copy, step, sign):
        for number in range(len(OFFSETS)):
            @pl.when(inside(me - sign * OFFSETS[number]))
            def _():
                copy(step, number).wait_recv()

    def wait_departures(copy, step, sign):
        for number in range(len(OFFSETS)):
            @pl.when(inside(me + sign * OFFSETS[number]))
            def _():
                copy(step, number).wait_send()

    stage_forward(0, pixels)
    pl.semaphore_wait(barrier, peers)
    start_all(copy_forward, 0, 1)

    ext0[pl.ds(0, blocks)] = pixels[...]
    part_f[0] = jnp.zeros(part_f.shape[1:], jnp.float32)
    part_b[0] = jnp.zeros(part_b.shape[1:], jnp.float32)
    part_a[0] = jnp.zeros(part_a.shape[1:], jnp.float32)
    count = live[0]
    live_target = [jnp.where(t < count, target[t], blocks) for t in range(max_tiles)]
    live_source = [jnp.where(t < count, source[t], ext_count) for t in range(max_tiles)]
    order_slots(live_source, ext_count, perm_b, keep_b, last_b)
    order_slots([chosen[t] for t in range(len(OFFSETS) * sends)], blocks, perm_a, keep_a, last_a)
    order_slots(live_target, blocks, perm_f, keep_f, last_f)

    for b in range(blocks):
        cot_t[:, b * size : (b + 1) * size] = (
            cotangent[b].astype(jnp.float32).T.astype(jnp.bfloat16)
        )

    group = GROUP if max_tiles % GROUP == 0 else 1

    def scan_tiles(product, perm, keep, part):
        def body(step, total):
            for inner in range(group):
                place = step * group + inner
                total = product(perm[place]) + keep[place] * total
                part[place + 1] = total
            return total

        lax.fori_loop(0, max_tiles // group, body, jnp.zeros(part.shape[1:], jnp.float32))

    def forward(step):
        def product(t):
            return jnp.dot(
                tiles[t], exts[step][source[t]], preferred_element_type=jnp.float32
            )

        scan_tiles(product, perm_f, keep_f, part_f)

    def transposed(step):
        def product(t):
            return jnp.dot(u[target[t]], tiles[t], preferred_element_type=jnp.float32)

        scan_tiles(product, perm_b, keep_b, part_b)
        for slot in range(ext_count - blocks):
            outs_b[step][slot] = part_b[last_b[blocks + slot]].astype(jnp.bfloat16)
        start_all(copy_backward, step, -1)

    def add_arrivals(step):
        wait_arrivals(copy_backward, step, -1)
        total = jnp.zeros((channels, size), jnp.float32)
        for place in range(len(OFFSETS) * sends):
            total = ins_b[step][perm_a[place]].astype(jnp.float32) + keep_a[place] * total
            part_a[place + 1] = total

    def pulled(order, b):
        return jnp.dot(
            filters[order], cot_t[:, b * size : (b + 1) * size],
            preferred_element_type=jnp.float32,
        )

    def gradient(order, member):
        found = jnp.dot(
            cot_t[...], member.reshape(blocks * size, channels),
            preferred_element_type=jnp.float32,
        )
        grads[pl.ds(order * channels, channels)] = found

    reducers = (
        (0, 3, red_send_a, red_land_a, red_out_a, red_slots_a, red_final_a),
        (3, 4, red_send_b, red_land_b, red_out_b, red_slots_b, red_final_b),
    )
    per_batch = 2 + sum(radix - 1 for radix in radices)

    def half_of(batch):
        return (reducers[batch][1] - reducers[batch][0]) * channels // 2

    def view_copy(batch, src, dst, sem):
        return pltpu.make_async_remote_copy(
            src_ref=src, dst_ref=dst,
            send_sem=r_send.at[batch, sem], recv_sem=r_recv.at[batch, sem],
            device_id={"view": 1 - view}, device_id_type=MESH,
        )

    def halves_copy(batch):
        return view_copy(batch, reducers[batch][2], reducers[batch][3], 0)

    def final_copy(batch):
        half = half_of(batch)
        mine = reducers[batch][6].at[pl.ds(pl.multiple_of(view * half, 16), half)]
        return view_copy(batch, mine, mine, 1)

    def group_copy(batch, level, shift):
        sem = 2 + sum(radix - 1 for radix in radices[:level]) + shift - 1
        return pltpu.make_async_remote_copy(
            src_ref=reducers[batch][4].at[level],
            dst_ref=reducers[batch][5].at[level, groups[level][2]],
            send_sem=r_send.at[batch, sem], recv_sem=r_recv.at[batch, sem],
            device_id={"sky": partner(groups[level], shift)}, device_id_type=MESH,
        )

    def send_halves(batch):
        first, half = reducers[batch][0] * channels, half_of(batch)
        theirs = pl.multiple_of(first + (1 - view) * half, 16)
        reducers[batch][2][...] = grads[pl.ds(theirs, half)].astype(jnp.bfloat16)
        halves_copy(batch).start()

    def send_level(batch, level, total):
        rounded = total.astype(jnp.bfloat16)
        reducers[batch][4][level] = rounded
        reducers[batch][5][level, groups[level][2]] = rounded
        for shift in range(1, radices[level]):
            group_copy(batch, level, shift).start()

    def sum_level(batch, level):
        for shift in range(1, radices[level]):
            group_copy(batch, level, shift).wait_recv()
        total = reducers[batch][5][level, 0].astype(jnp.float32)
        for spot in range(1, radices[level]):
            total = total + reducers[batch][5][level, spot].astype(jnp.float32)
        return total

    def reduce_step(batch, step):
        if step == 0:
            send_halves(batch)
            return
        if step == 1:
            halves_copy(batch).wait_recv()
            first, half = reducers[batch][0] * channels, half_of(batch)
            mine = pl.multiple_of(first + view * half, 16)
            total = grads[pl.ds(mine, half)] + reducers[batch][3][...].astype(jnp.float32)
        elif step <= 1 + len(radices):
            total = sum_level(batch, step - 2)
        else:
            final_copy(batch).wait_recv()
            for order in range(reducers[batch][0], reducers[batch][1]):
                at = pl.ds((order - reducers[batch][0]) * channels, channels)
                filter_grad[order] = (reducers[batch][6][at] * scale).T
            return
        if step <= len(radices):
            send_level(batch, step - 1, total)
        else:
            half = half_of(batch)
            reducers[batch][6][pl.ds(pl.multiple_of(view * half, 16), half)] = total
            final_copy(batch).start()

    steps = 3 + len(radices)

    for b in range(blocks):
        value = pulled(3, b)
        adj_three[b] = value
        u[b] = value.astype(jnp.bfloat16)
    tile_copy.wait()
    transposed(0)
    for b in range(blocks):
        adj_two[b] = pulled(2, b) + 2.0 * part_b[last_b[b]]

    wait_arrivals(copy_forward, 0, 1)
    forward(0)
    for b in range(blocks):
        value = part_f[last_f[b]].astype(jnp.bfloat16)
        ext1[b] = value
        latest[b] = value
    stage_forward(1, latest)
    start_all(copy_forward, 1, 1)
    gradient(0, pixels[...])
    gradient(1, ext1[pl.ds(0, blocks)])

    add_arrivals(0)
    for b in range(blocks):
        value = adj_two[b] + 2.0 * part_a[last_a[b]]
        adj_two[b] = value
        u[b] = value.astype(jnp.bfloat16)
    transposed(1)
    for b in range(blocks):
        adj_one[b] = pulled(1, b) + 2.0 * part_b[last_b[b]] - adj_three[b]

    wait_arrivals(copy_forward, 1, 1)
    forward(1)
    for b in range(blocks):
        value = 2.0 * part_f[last_f[b]] - pixels[b].astype(jnp.float32)
        ext2[b] = value.astype(jnp.bfloat16)
        latest[b] = value.astype(jnp.bfloat16)
    stage_forward(2, latest)
    start_all(copy_forward, 2, 1)
    gradient(2, ext2[pl.ds(0, blocks)])
    reduce_step(0, 0)

    add_arrivals(1)
    for b in range(blocks):
        value = adj_one[b] + 2.0 * part_a[last_a[b]]
        adj_one[b] = value
        u[b] = value.astype(jnp.bfloat16)
    transposed(2)
    reduce_step(0, 1)
    for b in range(blocks):
        adj_zero[b] = pulled(0, b) + part_b[last_b[b]] - adj_two[b]

    wait_arrivals(copy_forward, 2, 1)
    forward(2)
    for b in range(blocks):
        value = 2.0 * part_f[last_f[b]] - ext1[b].astype(jnp.float32)
        latest[b] = value.astype(jnp.bfloat16)
    gradient(3, latest[...])
    reduce_step(1, 0)
    reduce_step(0, 2)
    reduce_step(1, 1)

    weights = filters[...].reshape(filters.shape[0] * channels, channels)
    for b in range(blocks):
        joined = jnp.concatenate([pixels[b], ext1[b], ext2[b], latest[b]], axis=1)
        outputs[b] = jnp.dot(joined, weights, preferred_element_type=jnp.float32).astype(
            jnp.bfloat16
        )
    for step in range(2, steps):
        if step > 2:
            reduce_step(0, step)
        reduce_step(1, step)

    add_arrivals(2)
    for b in range(blocks):
        value = adj_zero[b] + part_a[last_a[b]]
        pixel_grad[b] = value.T.astype(jnp.bfloat16)

    for step in range(3):
        wait_departures(copy_forward, step, 1)
        wait_departures(copy_backward, step, -1)
    for batch in range(2):
        halves_copy(batch).wait_send()
        for level in range(len(radices)):
            for shift in range(1, radices[level]):
                group_copy(batch, level, shift).wait_send()
        final_copy(batch).wait_send()


def per_device(
    sky_size, view_size,
    pixels, cotangent, filters, lap_tiles, tile_target, tile_source, tile_count, send_blocks
):
    _, max_tiles, size, _ = lap_tiles.shape
    rows, channels = pixels.shape[1:]
    orders = filters.shape[0]
    blocks = rows // size
    slots = send_blocks.shape[1] * send_blocks.shape[2]
    ext_count = blocks + slots
    radices = radices_of(sky_size)
    bf, f32 = jnp.bfloat16, jnp.float32
    vmem = functools.partial(pl.BlockSpec, memory_space=pltpu.VMEM)
    smem = functools.partial(pl.BlockSpec, memory_space=pltpu.SMEM)

    def reducer(count):
        half = count * channels // 2
        return [
            pltpu.VMEM((half, channels), bf),
            pltpu.VMEM((half, channels), bf),
            pltpu.VMEM((len(radices), half, channels), bf),
            pltpu.VMEM((len(radices), max(radices), half, channels), bf),
            pltpu.VMEM((2 * half, channels), f32),
        ]

    sems = 2 + sum(radix - 1 for radix in radices)
    scratch = (
        [pltpu.VMEM((max_tiles, size, size), bf)]
        + [pltpu.VMEM((ext_count, size, channels), bf)] * 3
        + [pltpu.VMEM((blocks, size, channels), bf)]
        + [pltpu.VMEM((slots, size, channels), bf)] * 3
        + [pltpu.VMEM((slots, channels, size), bf)] * 6
        + [pltpu.VMEM((channels, rows), bf), pltpu.VMEM((blocks, channels, size), bf)]
        + [pltpu.VMEM((blocks, channels, size), f32)] * 4
        + [
            pltpu.VMEM((max_tiles + 1, size, channels), f32),
            pltpu.VMEM((max_tiles + 1, channels, size), f32),
            pltpu.VMEM((slots + 1, channels, size), f32),
            pltpu.VMEM((orders * channels, channels), f32),
        ]
        + reducer(3)
        + reducer(1)
        + [pltpu.SMEM((max_tiles,), jnp.int32)] * 2
        + [pltpu.SMEM((slots,), jnp.int32)]
        + [pltpu.SMEM((max_tiles,), f32)] * 2
        + [pltpu.SMEM((slots,), f32)]
        + [
            pltpu.SMEM((blocks,), jnp.int32),
            pltpu.SMEM((ext_count,), jnp.int32),
            pltpu.SMEM((blocks,), jnp.int32),
        ]
        + [pltpu.SemaphoreType.DMA]
        + [pltpu.SemaphoreType.DMA((3, len(OFFSETS)))] * 4
        + [pltpu.SemaphoreType.DMA((2, sems))] * 2
    )
    scale = 1.0 / math.sqrt(view_size * sky_size * rows)
    flops = 2 * channels * (6 * max_tiles * size * size + 3 * orders * rows * channels)
    outputs, pixel_grad, filter_grad = pl.pallas_call(
        functools.partial(kernel, sky_size, scale),
        out_shape=(
            jax.ShapeDtypeStruct((blocks, size, channels), bf),
            jax.ShapeDtypeStruct((blocks, size, channels), bf),
            jax.ShapeDtypeStruct((orders, channels, channels), f32),
        ),
        in_specs=[vmem()] * 3 + [smem()] * 4 + [pl.BlockSpec(memory_space=pl.ANY)],
        out_specs=(vmem(),) * 3,
        scratch_shapes=scratch,
        cost_estimate=pl.CostEstimate(
            flops=flops, bytes_accessed=2 * max_tiles * size * size, transcendentals=0
        ),
        compiler_params=pltpu.CompilerParams(
            collective_id=0, has_side_effects=True, vmem_limit_bytes=48 * 1024 * 1024
        ),
    )(
        pixels.reshape(blocks, size, channels),
        cotangent.reshape(blocks, size, channels),
        filters,
        tile_target.reshape(max_tiles),
        tile_source.reshape(max_tiles),
        tile_count,
        send_blocks.reshape(slots),
        lap_tiles.reshape(max_tiles, size, size),
    )
    return (
        outputs.reshape(1, rows, channels),
        pixel_grad.reshape(1, rows, channels),
        filter_grad,
    )


def solution(mesh):
    return jax.shard_map(
        functools.partial(per_device, mesh.shape["sky"], mesh.shape["view"]),
        mesh=mesh,
        in_specs=(
            P("view", "sky", None),
            P("view", "sky", None),
            P(),
            P("sky", None, None, None),
            P("sky", None),
            P("sky", None),
            P("sky"),
            P("sky", None, None),
        ),
        out_specs=(P("view", "sky", None), P("view", "sky", None), P()),
        check_vma=False,
    )
```

time: 395 us -> 85.1 us (0.22); the launches traced: 390 us -> 84.8 us
  waiting for transfers between devices: 140 us -> 0 us
  local copies, waits for them, and re-layouts: 95.7 us -> 9.33 us
  Pallas kernels: 0 us -> 74.2 us
  starting transfers between devices: 69.9 us -> 0 us
  matrix products: 64.3 us -> 0 us
  between operations: 15.5 us -> 1.29 us
  other arithmetic: 5.03 us -> 0 us
    psum x1 -> x0, waiting for transfers between devices: 133 us -> none  [per_device(): stacked = lax.psum(jnp.stack(grad_terms), ('view', 'sky'))]
    pallas_call x0 -> x1, Pallas kernels: none -> 74.2 us  [per_device(): pl.pallas_call(functools.partial(kernel, sky_size, scale), out_shape=(jax...]
    ppermute x24 -> x0, starting transfers between devices: 69.8 us -> none  [passed_along(): return lax.ppermute(array, axis, pairs)]
    dot_general x36 -> x0, matrix products: 64.3 us -> none  [the longest x6 21 us: tile_products(): jnp.einsum(contraction, tile_set, picked, preferred_element_type=jnp.floa...]
    gather x26 -> x0, local copies, waits for them, and re-layouts: 45.9 us -> none  [the longest x20 26.8 us: forward_pieces(): return [blocks[chosen[number]] for number in range(4)]]
    concatenate x5 -> x0, local copies, waits for them, and re-layouts: 18.5 us -> none  [forward_finish(): extended = jnp.concatenate([blocks] + arrived, axis=0)]
    dot_general x6 -> x0, local copies, waits for them, and re-layouts: 16.5 us -> none  [tile_products(): jnp.einsum(contraction, tile_set, picked, preferred_element_type=jnp.floa...]
    ppermute x24 -> x0, waiting for transfers between devices: 6.41 us -> none  [passed_along(): return lax.ppermute(array, axis, pairs)]
  transfers between devices with their start and end apart: 25 -> 0, of which waited for: 3 -> 0; matrix products, arithmetic and copies ran while one was open for 24% -> 0% of each run, Pallas kernels for 0% -> 0%
where the time goes in v1:
time: 85.1 us; the launch traced here: 84.8 us
  Pallas kernels  74.2 us (87%)
  local copies, waits for them, and re-layouts  9.33 us (11%)
  between operations  1.29 us (2%)
    pallas_call x1, Pallas kernels, per_device(): pl.pallas_call(functools.partial(kernel, sky_size, scale), out_shape=(jax...  74.2 us
    unnamed x16, local copies, waits for them, and re-layouts  9.24 us

profile of v1, /device:TPU:1, one launch (start us, length us, event | category | flops | bytes accessed | tf_op | source)
XLA Modules:
  0.0 84.8 jit_solution(13366278989374056565)
XLA Ops:
  1.3 0.8 copy.12
  2.0 0.1 reshape.34.chosen
  2.1 0.0 copy-start
  2.1 1.9 %copy-done = bf16[1,24,256,256]{3,2,1,0:T(8,128)(2,1)S(1)} copy-done((bf16[1,24,256,256]{3,2,1,0:T(8,128)(2,1)S(1)}, bf16[1,24,256,256]{3,2,1,0:T(8,128)(2,1)}, u32[]{:S(2)}) %copy-start) | copy-done | bytes 3145752
  4.0 0.0 copy-start.1
  4.0 1.0 %copy-done.1 = bf16[1,2048,128]{2,1,0:T(8,128)(2,1)S(1)} copy-done((bf16[1,2048,128]{2,1,0:T(8,128)(2,1)S(1)}, bf16[1,2048,128]{2,1,0:T(8,128)(2,1)}, u32[]{:S(2)}) %copy-start.1) | copy-done | bytes 524312
  5.1 0.0 copy-start.2
  5.1 1.0 %copy-done.2 = bf16[1,2048,128]{2,1,0:T(8,128)(2,1)S(1)} copy-done((bf16[1,2048,128]{2,1,0:T(8,128)(2,1)S(1)}, bf16[1,2048,128]{2,1,0:T(8,128)(2,1)}, u32[]{:S(2)}) %copy-start.2) | copy-done | bytes 524312
  6.1 0.0 copy-start.3
  6.1 0.9 %copy-done.3 = bf16[4,128,128]{2,1,0:T(8,128)(2,1)S(1)} copy-done((bf16[4,128,128]{2,1,0:T(8,128)(2,1)S(1)}, bf16[4,128,128]{2,1,0:T(8,128)(2,1)}, u32[]{:S(2)}) %copy-start.3) | copy-done | bytes 131096
  7.0 0.0 copy-start.4
  7.0 0.7 copy-done.4
  7.7 0.0 copy-start.5
  7.7 0.7 copy-done.5
  8.3 74.2 %shard_map.103 = (bf16[8,256,128]{2,1,0:T(8,128)(2,1)S(1)}, bf16[8,256,128]{2,1,0:T(8,128)(2,1)S(1)}, f32[4,128,128]{2,1,0:T(8,128)S(1)}) custom-call(bf16[8,256,128]{2,1,0:T(8,128)(2,1)S(1)} %bitcast.10, bf16[8,256,128]{2,1,0:T(8,128)(2,1)S(1)} %bitcast.11, bf16[4,128,128]{2,1,0:T(8,128)(2,1)S(1)} %copy-done.3, s32[24]{0:T(128)S(1)} %bitcast.12, ...), custom_call_target="tpu_custom_call" | custom-call | flops 3221225472 | bytes 3145728 | tf_op jit(solution)/shard_map/pallas_call | solution.py:461
  82.5 0.8 copy.17
  83.3 0.8 copy.18
  84.1 0.7 copy.19
Async XLA Ops:
  2.1 1.9 %copy-start = (bf16[1,24,256,256]{3,2,1,0:T(8,128)(2,1)S(1)}, bf16[1,24,256,256]{3,2,1,0:T(8,128)(2,1)}, u32[]{:S(2)}) copy-start(bf16[1,24,256,256]{3,2,1,0:T(8,128)(2,1)} %param.11) | copy-start | bytes 9437188
  4.0 1.0 %copy-start.1 = (bf16[1,2048,128]{2,1,0:T(8,128)(2,1)S(1)}, bf16[1,2048,128]{2,1,0:T(8,128)(2,1)}, u32[]{:S(2)}) copy-start(bf16[1,2048,128]{2,1,0:T(8,128)(2,1)} %param.8) | copy-start | bytes 1572868
  5.1 1.0 %copy-start.2 = (bf16[1,2048,128]{2,1,0:T(8,128)(2,1)S(1)}, bf16[1,2048,128]{2,1,0:T(8,128)(2,1)}, u32[]{:S(2)}) copy-start(bf16[1,2048,128]{2,1,0:T(8,128)(2,1)} %param.9) | copy-start | bytes 1572868
  6.1 0.9 %copy-start.3 = (bf16[4,128,128]{2,1,0:T(8,128)(2,1)S(1)}, bf16[4,128,128]{2,1,0:T(8,128)(2,1)}, u32[]{:S(2)}) copy-start(bf16[4,128,128]{2,1,0:T(8,128)(2,1)} %filters.1) | copy-start | bytes 393220
  7.0 0.7 copy-start.4
  7.7 0.7 copy-start.5

commit v2 on v1

--- a/solution.py
+++ b/solution.py
@@ -55,15 +55,16 @@
 
 def kernel(
     sky_size, scale,
-    pixels, cotangent, filters, target, source, live, chosen, tiles_hbm,
-    outputs, pixel_grad, filter_grad,
+    pixels_in, cotangent_in, filters_in, target, source, live, chosen, tiles_in,
+    outputs_out, pixel_grad_out, filter_grad_out,
+    pixels, cotangent, filters, outputs, pixel_grad, filter_grad,
     tiles, ext0, ext1, ext2, latest, out_f0, out_f1, out_f2, out_b0, out_b1, out_b2,
     in_b0, in_b1, in_b2, cot_t, u, adj_three, adj_two, adj_one, adj_zero,
     part_f, part_b, part_a, grads,
     red_send_a, red_land_a, red_out_a, red_slots_a, red_final_a,
     red_send_b, red_land_b, red_out_b, red_slots_b, red_final_b,
     perm_f, perm_b, perm_a, keep_f, keep_b, keep_a, last_f, last_b, last_a,
-    tile_sem, f_send, f_recv, b_send, b_recv, r_send, r_recv,
+    in_sem, out_sem, f_send, f_recv, b_send, b_recv, r_send, r_recv,
 ):
     me = lax.axis_index("sky")
     view = lax.axis_index("view")
@@ -75,8 +76,24 @@
     exts, outs_f = (ext0, ext1, ext2), (out_f0, out_f1, out_f2)
     outs_b, ins_b = (out_b0, out_b1, out_b2), (in_b0, in_b1, in_b2)
 
-    tile_copy = pltpu.make_async_copy(tiles_hbm, tiles, tile_sem)
-    tile_copy.start()
+    loads = [
+        pltpu.make_async_copy(src, dst, in_sem.at[number])
+        for number, (src, dst) in enumerate((
+            (pixels_in, pixels),
+            (cotangent_in, cotangent),
+            (filters_in, filters),
+            (pixels_in, ext0.at[pl.ds(0, blocks)]),
+            (tiles_in, tiles),
+        ))
+    ]
+    stores = [
+        pltpu.make_async_copy(src, dst, out_sem.at[number])
+        for number, (src, dst) in enumerate((
+            (outputs, outputs_out), (filter_grad, filter_grad_out), (pixel_grad, pixel_grad_out)
+        ))
+    ]
+    for load in loads:
+        load.start()
 
     def inside(place):
         return jnp.logical_and(place >= 0, place < sky_size)
@@ -165,11 +182,11 @@
             def _():
                 copy(step, number).wait_send()
 
+    loads[0].wait()
     stage_forward(0, pixels)
     pl.semaphore_wait(barrier, peers)
     start_all(copy_forward, 0, 1)
 
-    ext0[pl.ds(0, blocks)] = pixels[...]
     part_f[0] = jnp.zeros(part_f.shape[1:], jnp.float32)
     part_b[0] = jnp.zeros(part_b.shape[1:], jnp.float32)
     part_a[0] = jnp.zeros(part_a.shape[1:], jnp.float32)
@@ -180,6 +197,7 @@
     order_slots([chosen[t] for t in range(len(OFFSETS) * sends)], blocks, perm_a, keep_a, last_a)
     order_slots(live_target, blocks, perm_f, keep_f, last_f)
 
+    loads[1].wait()
     for b in range(blocks):
         cot_t[:, b * size : (b + 1) * size] = (
             cotangent[b].astype(jnp.float32).T.astype(jnp.bfloat16)
@@ -314,15 +332,17 @@
 
     steps = 3 + len(radices)
 
+    loads[2].wait()
     for b in range(blocks):
         value = pulled(3, b)
         adj_three[b] = value
         u[b] = value.astype(jnp.bfloat16)
-    tile_copy.wait()
+    loads[4].wait()
     transposed(0)
     for b in range(blocks):
         adj_two[b] = pulled(2, b) + 2.0 * part_b[last_b[b]]
 
+    loads[3].wait()
     wait_arrivals(copy_forward, 0, 1)
     forward(0)
     for b in range(blocks):
@@ -380,15 +400,18 @@
         outputs[b] = jnp.dot(joined, weights, preferred_element_type=jnp.float32).astype(
             jnp.bfloat16
         )
+    stores[0].start()
     for step in range(2, steps):
         if step > 2:
             reduce_step(0, step)
         reduce_step(1, step)
+    stores[1].start()
 
     add_arrivals(2)
     for b in range(blocks):
         value = adj_zero[b] + part_a[last_a[b]]
         pixel_grad[b] = value.T.astype(jnp.bfloat16)
+    stores[2].start()
 
     for step in range(3):
         wait_departures(copy_forward, step, 1)
@@ -399,6 +422,8 @@
             for shift in range(1, radices[level]):
                 group_copy(batch, level, shift).wait_send()
         final_copy(batch).wait_send()
+    for store in stores:
+        store.wait()
 
 
 def per_device(
@@ -413,7 +438,7 @@
     ext_count = blocks + slots
     radices = radices_of(sky_size)
     bf, f32 = jnp.bfloat16, jnp.float32
-    vmem = functools.partial(pl.BlockSpec, memory_space=pltpu.VMEM)
+    anywhere = pl.BlockSpec(memory_space=pl.ANY)
     smem = functools.partial(pl.BlockSpec, memory_space=pltpu.SMEM)
 
     def reducer(count):
@@ -428,7 +453,11 @@
 
     sems = 2 + sum(radix - 1 for radix in radices)
     scratch = (
-        [pltpu.VMEM((max_tiles, size, size), bf)]
+        [pltpu.VMEM((blocks, size, channels), bf)] * 2
+        + [pltpu.VMEM((orders, channels, channels), bf)]
+        + [pltpu.VMEM((blocks, size, channels), bf)] * 2
+        + [pltpu.VMEM((orders, channels, channels), f32)]
+        + [pltpu.VMEM((max_tiles, size, size), bf)]
         + [pltpu.VMEM((ext_count, size, channels), bf)] * 3
         + [pltpu.VMEM((blocks, size, channels), bf)]
         + [pltpu.VMEM((slots, size, channels), bf)] * 3
@@ -452,7 +481,7 @@
             pltpu.SMEM((ext_count,), jnp.int32),
             pltpu.SMEM((blocks,), jnp.int32),
         ]
-        + [pltpu.SemaphoreType.DMA]
+        + [pltpu.SemaphoreType.DMA((5,)), pltpu.SemaphoreType.DMA((3,))]
         + [pltpu.SemaphoreType.DMA((3, len(OFFSETS)))] * 4
         + [pltpu.SemaphoreType.DMA((2, sems))] * 2
     )
@@ -465,14 +494,14 @@
             jax.ShapeDtypeStruct((blocks, size, channels), bf),
             jax.ShapeDtypeStruct((orders, channels, channels), f32),
         ),
-        in_specs=[vmem()] * 3 + [smem()] * 4 + [pl.BlockSpec(memory_space=pl.ANY)],
-        out_specs=(vmem(),) * 3,
+        in_specs=[anywhere] * 3 + [smem()] * 4 + [anywhere],
+        out_specs=(anywhere,) * 3,
         scratch_shapes=scratch,
         cost_estimate=pl.CostEstimate(
             flops=flops, bytes_accessed=2 * max_tiles * size * size, transcendentals=0
         ),
         compiler_params=pltpu.CompilerParams(
-            collective_id=0, has_side_effects=True, vmem_limit_bytes=48 * 1024 * 1024
+            collective_id=0, has_side_effects=True, vmem_limit_bytes=60 * 1024 * 1024
         ),
     )(
         pixels.reshape(blocks, size, channels),

time: 85.1 us -> 83.2 us (0.978)
  local copies, waits for them, and re-layouts: 9.33 us -> 6.77 us
    unnamed x16 -> x4, local copies, waits for them, and re-layouts: 9.24 us -> 6.17 us
where the time goes in v2:
time: 83.2 us; the launch traced here: 83 us
  Pallas kernels  74.9 us (90%)
  local copies, waits for them, and re-layouts  6.77 us (8%)
  between operations  1.29 us (2%)
    pallas_call x1, Pallas kernels, per_device(): pl.pallas_call(functools.partial(kernel, sky_size, scale), out_shape=(jax...  74.9 us
    unnamed x4, local copies, waits for them, and re-layouts  6.17 us

profile of v2, /device:TPU:1, one launch (start us, length us, event | category | flops | bytes accessed | tf_op | source)
XLA Modules:
  0.0 83.0 jit_solution(5540809047531879296)
XLA Ops:
  1.3 0.8 copy.12
  2.0 0.6 reshape.34.chosen
  2.6 74.9 %shard_map.103 = (bf16[8,256,128]{2,1,0:T(8,128)(2,1)}, bf16[8,256,128]{2,1,0:T(8,128)(2,1)}, f32[4,128,128]{2,1,0:T(8,128)}) custom-call(bf16[8,256,128]{2,1,0:T(8,128)(2,1)} %bitcast.10, bf16[8,256,128]{2,1,0:T(8,128)(2,1)} %bitcast.11, bf16[4,128,128]{2,1,0:T(8,128)(2,1)} %filters_in.1, s32[24]{0:T(128)} %bitcast.12, s32[24]{0:T(128)} %bitcast.13, ...), custom_call_target="tpu_custom_call" | custom-call | flops 3221225472 | bytes 3145728 | tf_op jit(solution)/shard_map/pallas_call | solution.py:490
  77.6 1.9 %copy.17 = bf16[1,2048,128]{2,1,0:T(8,128)(2,1)} copy(bf16[1,2048,128]{2,1,0:T(8,128)(2,1)} %bitcast.8) | data formatting | bytes 1048576
  79.4 1.9 %copy.18 = bf16[1,2048,128]{2,1,0:T(8,128)(2,1)} copy(bf16[1,2048,128]{2,1,0:T(8,128)(2,1)} %bitcast.7) | data formatting | bytes 1048576
  81.3 1.7 %copy.19 = f32[4,128,128]{2,1,0:T(8,128)} copy(f32[4,128,128]{2,1,0:T(8,128)} %get-tuple-element.14) | data formatting | bytes 524288

commit v3 on v2

--- a/solution.py
+++ b/solution.py
@@ -230,10 +230,11 @@
         scan_tiles(product, perm_b, keep_b, part_b)
         for slot in range(ext_count - blocks):
             outs_b[step][slot] = part_b[last_b[blocks + slot]].astype(jnp.bfloat16)
-        start_all(copy_backward, step, -1)
 
     def add_arrivals(step):
         wait_arrivals(copy_backward, step, -1)
+        if step < 2:
+            start_all(copy_forward, step + 1, 1)
         total = jnp.zeros((channels, size), jnp.float32)
         for place in range(len(OFFSETS) * sends):
             total = ins_b[step][perm_a[place]].astype(jnp.float32) + keep_a[place] * total
@@ -344,13 +345,13 @@
 
     loads[3].wait()
     wait_arrivals(copy_forward, 0, 1)
+    start_all(copy_backward, 0, -1)
     forward(0)
     for b in range(blocks):
         value = part_f[last_f[b]].astype(jnp.bfloat16)
         ext1[b] = value
         latest[b] = value
     stage_forward(1, latest)
-    start_all(copy_forward, 1, 1)
     gradient(0, pixels[...])
     gradient(1, ext1[pl.ds(0, blocks)])
 
@@ -364,13 +365,13 @@
         adj_one[b] = pulled(1, b) + 2.0 * part_b[last_b[b]] - adj_three[b]
 
     wait_arrivals(copy_forward, 1, 1)
+    start_all(copy_backward, 1, -1)
     forward(1)
     for b in range(blocks):
         value = 2.0 * part_f[last_f[b]] - pixels[b].astype(jnp.float32)
         ext2[b] = value.astype(jnp.bfloat16)
         latest[b] = value.astype(jnp.bfloat16)
     stage_forward(2, latest)
-    start_all(copy_forward, 2, 1)
     gradient(2, ext2[pl.ds(0, blocks)])
     reduce_step(0, 0)
 
@@ -385,6 +386,7 @@
         adj_zero[b] = pulled(0, b) + part_b[last_b[b]] - adj_two[b]
 
     wait_arrivals(copy_forward, 2, 1)
+    start_all(copy_backward, 2, -1)
     forward(2)
     for b in range(blocks):
         value = 2.0 * part_f[last_f[b]] - ext1[b].astype(jnp.float32)

time: 83.2 us -> 81 us (0.974)
  Pallas kernels: 74.9 us -> 72.7 us
    pallas_call x1, Pallas kernels: 74.9 us -> 72.7 us  [per_device(): pl.pallas_call(functools.partial(kernel, sky_size, scale), out_shape=(jax...]
where the time goes in v3:
time: 81 us; the launch traced here: 80.8 us
  Pallas kernels  72.7 us (90%)
  local copies, waits for them, and re-layouts  6.77 us (8%)
  between operations  1.29 us (2%)
    pallas_call x1, Pallas kernels, per_device(): pl.pallas_call(functools.partial(kernel, sky_size, scale), out_shape=(jax...  72.7 us
    unnamed x4, local copies, waits for them, and re-layouts  6.17 us

profile of v3, /device:TPU:1, one launch (start us, length us, event | category | flops | bytes accessed | tf_op | source)
XLA Modules:
  0.0 80.8 jit_solution(16614837915289703568)
XLA Ops:
  1.3 0.8 copy.12
  2.0 0.6 reshape.34.chosen
  2.6 72.7 %shard_map.103 = (bf16[8,256,128]{2,1,0:T(8,128)(2,1)}, bf16[8,256,128]{2,1,0:T(8,128)(2,1)}, f32[4,128,128]{2,1,0:T(8,128)}) custom-call(bf16[8,256,128]{2,1,0:T(8,128)(2,1)} %bitcast.10, bf16[8,256,128]{2,1,0:T(8,128)(2,1)} %bitcast.11, bf16[4,128,128]{2,1,0:T(8,128)(2,1)} %filters_in.1, s32[24]{0:T(128)} %bitcast.12, s32[24]{0:T(128)} %bitcast.13, ...), custom_call_target="tpu_custom_call" | custom-call | flops 3221225472 | bytes 3145728 | tf_op jit(solution)/shard_map/pallas_call | solution.py:492
  75.3 1.9 %copy.17 = bf16[1,2048,128]{2,1,0:T(8,128)(2,1)} copy(bf16[1,2048,128]{2,1,0:T(8,128)(2,1)} %bitcast.8) | data formatting | bytes 1048576
  77.2 1.9 %copy.18 = bf16[1,2048,128]{2,1,0:T(8,128)(2,1)} copy(bf16[1,2048,128]{2,1,0:T(8,128)(2,1)} %bitcast.7) | data formatting | bytes 1048576
  79.1 1.7 %copy.19 = f32[4,128,128]{2,1,0:T(8,128)} copy(f32[4,128,128]{2,1,0:T(8,128)} %get-tuple-element.14) | data formatting | bytes 524288

commit v4 on v2

--- a/solution.py
+++ b/solution.py
@@ -55,16 +55,16 @@
 
 def kernel(
     sky_size, scale,
-    pixels_in, cotangent_in, filters_in, target, source, live, chosen, tiles_in,
-    outputs_out, pixel_grad_out, filter_grad_out,
-    pixels, cotangent, filters, outputs, pixel_grad, filter_grad,
+    pixels_in, cotangent_in, filters_in, target_in, source_in, live, chosen, tiles_in,
+    outputs, pixel_grad, filter_grad,
+    target, source, pixels, cotangent, filters,
     tiles, ext0, ext1, ext2, latest, out_f0, out_f1, out_f2, out_b0, out_b1, out_b2,
     in_b0, in_b1, in_b2, cot_t, u, adj_three, adj_two, adj_one, adj_zero,
     part_f, part_b, part_a, grads,
     red_send_a, red_land_a, red_out_a, red_slots_a, red_final_a,
     red_send_b, red_land_b, red_out_b, red_slots_b, red_final_b,
     perm_f, perm_b, perm_a, keep_f, keep_b, keep_a, last_f, last_b, last_a,
-    in_sem, out_sem, f_send, f_recv, b_send, b_recv, r_send, r_recv,
+    in_sem, f_send, f_recv, b_send, b_recv, r_send, r_recv,
 ):
     me = lax.axis_index("sky")
     view = lax.axis_index("view")
@@ -84,12 +84,8 @@
             (filters_in, filters),
             (pixels_in, ext0.at[pl.ds(0, blocks)]),
             (tiles_in, tiles),
-        ))
-    ]
-    stores = [
-        pltpu.make_async_copy(src, dst, out_sem.at[number])
-        for number, (src, dst) in enumerate((
-            (outputs, outputs_out), (filter_grad, filter_grad_out), (pixel_grad, pixel_grad_out)
+            (target_in, target),
+            (source_in, source),
         ))
     ]
     for load in loads:
@@ -137,12 +133,12 @@
         def _():
             for landed in ins_b:
                 landed[pl.ds(number * sends, sends)] = jnp.zeros(
-                    (sends, channels, size), jnp.bfloat16
+                    (sends,) + landed.shape[1:], jnp.bfloat16
                 )
 
     def stage_forward(step, blocks_ref):
         for slot in range(len(OFFSETS) * sends):
-            outs_f[step][slot] = blocks_ref[chosen[slot]]
+            outs_f[step][slot] = blocks_ref[chosen[0, slot // sends, slot % sends]]
 
     def copy_forward(step, number):
         return pltpu.make_async_remote_copy(
@@ -190,11 +186,16 @@
     part_f[0] = jnp.zeros(part_f.shape[1:], jnp.float32)
     part_b[0] = jnp.zeros(part_b.shape[1:], jnp.float32)
     part_a[0] = jnp.zeros(part_a.shape[1:], jnp.float32)
+    loads[5].wait()
+    loads[6].wait()
     count = live[0]
     live_target = [jnp.where(t < count, target[t], blocks) for t in range(max_tiles)]
     live_source = [jnp.where(t < count, source[t], ext_count) for t in range(max_tiles)]
     order_slots(live_source, ext_count, perm_b, keep_b, last_b)
-    order_slots([chosen[t] for t in range(len(OFFSETS) * sends)], blocks, perm_a, keep_a, last_a)
+    order_slots(
+        [chosen[0, t // sends, t % sends] for t in range(len(OFFSETS) * sends)],
+        blocks, perm_a, keep_a, last_a,
+    )
     order_slots(live_target, blocks, perm_f, keep_f, last_f)
 
     loads[1].wait()
@@ -229,15 +230,19 @@
 
         scan_tiles(product, perm_b, keep_b, part_b)
         for slot in range(ext_count - blocks):
-            outs_b[step][slot] = part_b[last_b[blocks + slot]].astype(jnp.bfloat16)
-        start_all(copy_backward, step, -1)
+            value = part_b[last_b[blocks + slot]]
+            outs_b[step][slot] = (value.T if step == 2 else value).astype(jnp.bfloat16)
 
     def add_arrivals(step):
+        if step < 2:
+            wait_departures(copy_backward, step, -1)
+            start_all(copy_forward, step + 1, 1)
         wait_arrivals(copy_backward, step, -1)
-        total = jnp.zeros((channels, size), jnp.float32)
+        part = part_f if step == 2 else part_a
+        total = jnp.zeros(part.shape[1:], jnp.float32)
         for place in range(len(OFFSETS) * sends):
             total = ins_b[step][perm_a[place]].astype(jnp.float32) + keep_a[place] * total
-            part_a[place + 1] = total
+            part[place + 1] = total
 
     def pulled(order, b):
         return jnp.dot(
@@ -343,6 +348,8 @@
         adj_two[b] = pulled(2, b) + 2.0 * part_b[last_b[b]]
 
     loads[3].wait()
+    wait_departures(copy_forward, 0, 1)
+    start_all(copy_backward, 0, -1)
     wait_arrivals(copy_forward, 0, 1)
     forward(0)
     for b in range(blocks):
@@ -350,7 +357,6 @@
         ext1[b] = value
         latest[b] = value
     stage_forward(1, latest)
-    start_all(copy_forward, 1, 1)
     gradient(0, pixels[...])
     gradient(1, ext1[pl.ds(0, blocks)])
 
@@ -363,6 +369,8 @@
     for b in range(blocks):
         adj_one[b] = pulled(1, b) + 2.0 * part_b[last_b[b]] - adj_three[b]
 
+    wait_departures(copy_forward, 1, 1)
+    start_all(copy_backward, 1, -1)
     wait_arrivals(copy_forward, 1, 1)
     forward(1)
     for b in range(blocks):
@@ -370,7 +378,6 @@
         ext2[b] = value.astype(jnp.bfloat16)
         latest[b] = value.astype(jnp.bfloat16)
     stage_forward(2, latest)
-    start_all(copy_forward, 2, 1)
     gradient(2, ext2[pl.ds(0, blocks)])
     reduce_step(0, 0)
 
@@ -382,8 +389,10 @@
     transposed(2)
     reduce_step(0, 1)
     for b in range(blocks):
-        adj_zero[b] = pulled(0, b) + part_b[last_b[b]] - adj_two[b]
-
+        adj_zero[b] = (pulled(0, b) + part_b[last_b[b]] - adj_two[b]).T
+
+    wait_departures(copy_forward, 2, 1)
+    start_all(copy_backward, 2, -1)
     wait_arrivals(copy_forward, 2, 1)
     forward(2)
     for b in range(blocks):
@@ -400,30 +409,26 @@
         outputs[b] = jnp.dot(joined, weights, preferred_element_type=jnp.float32).astype(
             jnp.bfloat16
         )
-    stores[0].start()
     for step in range(2, steps):
         if step > 2:
             reduce_step(0, step)
         reduce_step(1, step)
-    stores[1].start()
 
     add_arrivals(2)
     for b in range(blocks):
-        value = adj_zero[b] + part_a[last_a[b]]
-        pixel_grad[b] = value.T.astype(jnp.bfloat16)
-    stores[2].start()
-
-    for step in range(3):
-        wait_departures(copy_forward, step, 1)
-        wait_departures(copy_backward, step, -1)
+        pixel_grad[b] = (adj_zero[b] + part_f[last_a[b]]).astype(jnp.bfloat16)
+
+    wait_departures(copy_backward, 2, -1)
     for batch in range(2):
         halves_copy(batch).wait_send()
         for level in range(len(radices)):
             for shift in range(1, radices[level]):
                 group_copy(batch, level, shift).wait_send()
         final_copy(batch).wait_send()
-    for store in stores:
-        store.wait()
+
+
+def in_hbm(array):
+    return pltpu.with_memory_space_constraint(array, pltpu.HBM)
 
 
 def per_device(
@@ -438,7 +443,7 @@
     ext_count = blocks + slots
     radices = radices_of(sky_size)
     bf, f32 = jnp.bfloat16, jnp.float32
-    anywhere = pl.BlockSpec(memory_space=pl.ANY)
+    outside = pl.BlockSpec(memory_space=pltpu.HBM)
     smem = functools.partial(pl.BlockSpec, memory_space=pltpu.SMEM)
 
     def reducer(count):
@@ -453,17 +458,20 @@
 
     sems = 2 + sum(radix - 1 for radix in radices)
     scratch = (
-        [pltpu.VMEM((blocks, size, channels), bf)] * 2
+        [pltpu.SMEM((max_tiles,), jnp.int32)] * 2
+        + [pltpu.VMEM((blocks, size, channels), bf)] * 2
         + [pltpu.VMEM((orders, channels, channels), bf)]
-        + [pltpu.VMEM((blocks, size, channels), bf)] * 2
-        + [pltpu.VMEM((orders, channels, channels), f32)]
         + [pltpu.VMEM((max_tiles, size, size), bf)]
         + [pltpu.VMEM((ext_count, size, channels), bf)] * 3
         + [pltpu.VMEM((blocks, size, channels), bf)]
         + [pltpu.VMEM((slots, size, channels), bf)] * 3
-        + [pltpu.VMEM((slots, channels, size), bf)] * 6
+        + [pltpu.VMEM((slots, channels, size), bf)] * 2
+        + [pltpu.VMEM((slots, size, channels), bf)]
+        + [pltpu.VMEM((slots, channels, size), bf)] * 2
+        + [pltpu.VMEM((slots, size, channels), bf)]
         + [pltpu.VMEM((channels, rows), bf), pltpu.VMEM((blocks, channels, size), bf)]
-        + [pltpu.VMEM((blocks, channels, size), f32)] * 4
+        + [pltpu.VMEM((blocks, channels, size), f32)] * 3
+        + [pltpu.VMEM((blocks, size, channels), f32)]
         + [
             pltpu.VMEM((max_tiles + 1, size, channels), f32),
             pltpu.VMEM((max_tiles + 1, channels, size), f32),
@@ -481,7 +489,7 @@
             pltpu.SMEM((ext_count,), jnp.int32),
             pltpu.SMEM((blocks,), jnp.int32),
         ]
-        + [pltpu.SemaphoreType.DMA((5,)), pltpu.SemaphoreType.DMA((3,))]
+        + [pltpu.SemaphoreType.DMA((7,))]
         + [pltpu.SemaphoreType.DMA((3, len(OFFSETS)))] * 4
         + [pltpu.SemaphoreType.DMA((2, sems))] * 2
     )
@@ -494,24 +502,24 @@
             jax.ShapeDtypeStruct((blocks, size, channels), bf),
             jax.ShapeDtypeStruct((orders, channels, channels), f32),
         ),
-        in_specs=[anywhere] * 3 + [smem()] * 4 + [anywhere],
-        out_specs=(anywhere,) * 3,
+        in_specs=[outside] * 5 + [smem()] * 2 + [outside],
+        out_specs=(pl.BlockSpec(memory_space=pltpu.VMEM),) * 3,
         scratch_shapes=scratch,
         cost_estimate=pl.CostEstimate(
             flops=flops, bytes_accessed=2 * max_tiles * size * size, transcendentals=0
         ),
         compiler_params=pltpu.CompilerParams(
-            collective_id=0, has_side_effects=True, vmem_limit_bytes=60 * 1024 * 1024
+            collective_id=0, has_side_effects=True, vmem_limit_bytes=48 * 1024 * 1024
         ),
     )(
-        pixels.reshape(blocks, size, channels),
-        cotangent.reshape(blocks, size, channels),
-        filters,
-        tile_target.reshape(max_tiles),
-        tile_source.reshape(max_tiles),
+        in_hbm(pixels.reshape(blocks, size, channels)),
+        in_hbm(cotangent.reshape(blocks, size, channels)),
+        in_hbm(filters),
+        in_hbm(tile_target.reshape(max_tiles)),
+        in_hbm(tile_source.reshape(max_tiles)),
         tile_count,
-        send_blocks.reshape(slots),
-        lap_tiles.reshape(max_tiles, size, size),
+        send_blocks,
+        in_hbm(lap_tiles.reshape(max_tiles, size, size)),
     )
     return (
         outputs.reshape(1, rows, channels),

time: 83.2 us -> 74.9 us (0.900)
  Pallas kernels: 74.9 us -> 70.4 us
  local copies, waits for them, and re-layouts: 6.77 us -> 3.06 us
    pallas_call x1, Pallas kernels: 74.9 us -> 70.4 us  [per_device(): pl.pallas_call(functools.partial(kernel, sky_size, scale), out_shape=(jax...]
    unnamed x4, local copies, waits for them, and re-layouts: 6.17 us -> 3.06 us
where the time goes in v4:
time: 74.9 us; the launch traced here: 74.7 us
  Pallas kernels  70.4 us (94%)
  local copies, waits for them, and re-layouts  3.06 us (4%)
  between operations  1.29 us (2%)
    pallas_call x1, Pallas kernels, per_device(): pl.pallas_call(functools.partial(kernel, sky_size, scale), out_shape=(jax...  70.4 us
    unnamed x4, local copies, waits for them, and re-layouts  3.06 us

profile of v4, /device:TPU:1, one launch (start us, length us, event | category | flops | bytes accessed | tf_op | source)
XLA Modules:
  0.0 74.7 jit_solution(5204164498951053994)
XLA Ops:
  1.3 0.8 %copy.11.chosen = s32[1,4,2]{2,1,0:T(4,128)S(1)} copy(s32[1,4,2]{1,2,0:T(2,128)} %param.15) | data formatting | bytes 64 | tf_op args[7]
  2.0 70.4 %shard_map.103 = (bf16[8,256,128]{2,1,0:T(8,128)(2,1)S(1)}, bf16[8,256,128]{2,1,0:T(8,128)(2,1)S(1)}, f32[4,128,128]{2,1,0:T(8,128)S(1)}) custom-call(bf16[8,256,128]{2,1,0:T(8,128)(2,1)} %bitcast.10, bf16[8,256,128]{2,1,0:T(8,128)(2,1)} %bitcast.11, bf16[4,128,128]{2,1,0:T(8,128)(2,1)} %filters_in.1, s32[24]{0:T(128)} %bitcast.12, s32[24]{0:T(128)} %bitcast.13, ...), custom_call_target="tpu_custom_call" | custom-call | flops 3221225472 | bytes 3145728 | tf_op jit(solution)/shard_map/pallas_call | solution.py:498
  72.4 0.8 %copy.16 = bf16[1,2048,128]{2,1,0:T(8,128)(2,1)} copy(bf16[1,2048,128]{2,1,0:T(8,128)(2,1)S(1)} %bitcast.8) | data formatting | bytes 1048576
  73.2 0.8 %copy.17 = bf16[1,2048,128]{2,1,0:T(8,128)(2,1)} copy(bf16[1,2048,128]{2,1,0:T(8,128)(2,1)S(1)} %bitcast.7) | data formatting | bytes 1048576
  74.0 0.7 copy.18

commit v5 on v4

--- a/solution.py
+++ b/solution.py
@@ -12,7 +12,7 @@
 MESH = pl.DeviceIdType.MESH
 STRIDE = 64
 BIG = 1 << 20
-GROUP = 8
+GROUP = 12
 
 
 def radices_of(size):
@@ -172,6 +172,13 @@
             def _():
                 copy(step, number).wait_recv()
 
+    def hand_over(done, done_step, sign, copy, step):
+        for number in (3, 2, 1, 0):
+            @pl.when(inside(me + sign * OFFSETS[number]))
+            def _():
+                done(done_step, number).wait_send()
+                copy(step, number ^ 1).start()
+
     def wait_departures(copy, step, sign):
         for number in range(len(OFFSETS)):
             @pl.when(inside(me + sign * OFFSETS[number]))
@@ -235,8 +242,7 @@
 
     def add_arrivals(step):
         if step < 2:
-            wait_departures(copy_backward, step, -1)
-            start_all(copy_forward, step + 1, 1)
+            hand_over(copy_backward, step, -1, copy_forward, step + 1)
         wait_arrivals(copy_backward, step, -1)
         part = part_f if step == 2 else part_a
         total = jnp.zeros(part.shape[1:], jnp.float32)
@@ -348,8 +354,7 @@
         adj_two[b] = pulled(2, b) + 2.0 * part_b[last_b[b]]
 
     loads[3].wait()
-    wait_departures(copy_forward, 0, 1)
-    start_all(copy_backward, 0, -1)
+    hand_over(copy_forward, 0, 1, copy_backward, 0)
     wait_arrivals(copy_forward, 0, 1)
     forward(0)
     for b in range(blocks):
@@ -369,8 +374,7 @@
     for b in range(blocks):
         adj_one[b] = pulled(1, b) + 2.0 * part_b[last_b[b]] - adj_three[b]
 
-    wait_departures(copy_forward, 1, 1)
-    start_all(copy_backward, 1, -1)
+    hand_over(copy_forward, 1, 1, copy_backward, 1)
     wait_arrivals(copy_forward, 1, 1)
     forward(1)
     for b in range(blocks):
@@ -391,8 +395,7 @@
     for b in range(blocks):
         adj_zero[b] = (pulled(0, b) + part_b[last_b[b]] - adj_two[b]).T
 
-    wait_departures(copy_forward, 2, 1)
-    start_all(copy_backward, 2, -1)
+    hand_over(copy_forward, 2, 1, copy_backward, 2)
     wait_arrivals(copy_forward, 2, 1)
     forward(2)
     for b in range(blocks):

time: 74.9 us -> 73.7 us (0.984)
  Pallas kernels: 70.4 us -> 69.2 us
    pallas_call x1, Pallas kernels: 70.4 us -> 69.2 us  [per_device(): pl.pallas_call(functools.partial(kernel, sky_size, scale), out_shape=(jax...]
where the time goes in v5:
time: 73.7 us; the launch traced here: 73.6 us
  Pallas kernels  69.2 us (94%)
  local copies, waits for them, and re-layouts  3.06 us (4%)
  between operations  1.29 us (2%)
    pallas_call x1, Pallas kernels, per_device(): pl.pallas_call(functools.partial(kernel, sky_size, scale), out_shape=(jax...  69.2 us
    unnamed x4, local copies, waits for them, and re-layouts  3.06 us

profile of v5, /device:TPU:1, one launch (start us, length us, event | category | flops | bytes accessed | tf_op | source)
XLA Modules:
  0.0 73.6 jit_solution(17931455122631669772)
XLA Ops:
  1.3 0.8 %copy.11.chosen = s32[1,4,2]{2,1,0:T(4,128)S(1)} copy(s32[1,4,2]{1,2,0:T(2,128)} %param.15) | data formatting | bytes 64 | tf_op args[7]
  2.0 69.2 %shard_map.103 = (bf16[8,256,128]{2,1,0:T(8,128)(2,1)S(1)}, bf16[8,256,128]{2,1,0:T(8,128)(2,1)S(1)}, f32[4,128,128]{2,1,0:T(8,128)S(1)}) custom-call(bf16[8,256,128]{2,1,0:T(8,128)(2,1)} %bitcast.10, bf16[8,256,128]{2,1,0:T(8,128)(2,1)} %bitcast.11, bf16[4,128,128]{2,1,0:T(8,128)(2,1)} %filters_in.1, s32[24]{0:T(128)} %bitcast.12, s32[24]{0:T(128)} %bitcast.13, ...), custom_call_target="tpu_custom_call" | custom-call | flops 3221225472 | bytes 3145728 | tf_op jit(solution)/shard_map/pallas_call | solution.py:501
  71.3 0.8 %copy.16 = bf16[1,2048,128]{2,1,0:T(8,128)(2,1)} copy(bf16[1,2048,128]{2,1,0:T(8,128)(2,1)S(1)} %bitcast.8) | data formatting | bytes 1048576
  72.1 0.8 %copy.17 = bf16[1,2048,128]{2,1,0:T(8,128)(2,1)} copy(bf16[1,2048,128]{2,1,0:T(8,128)(2,1)S(1)} %bitcast.7) | data formatting | bytes 1048576
  72.8 0.7 copy.18

commit v6 on v5

--- a/solution.py
+++ b/solution.py
@@ -412,14 +412,16 @@
         outputs[b] = jnp.dot(joined, weights, preferred_element_type=jnp.float32).astype(
             jnp.bfloat16
         )
-    for step in range(2, steps):
+    for step in range(2, steps - 1):
         if step > 2:
             reduce_step(0, step)
         reduce_step(1, step)
+    reduce_step(0, steps - 1)
 
     add_arrivals(2)
     for b in range(blocks):
         pixel_grad[b] = (adj_zero[b] + part_f[last_a[b]]).astype(jnp.bfloat16)
+    reduce_step(1, steps - 1)
 
     wait_departures(copy_backward, 2, -1)
     for batch in range(2):

time: 73.7 us -> 73.5 us (level)
  no operation moved by 1% of the time
where the time goes in v6:
time: 73.5 us; the launch traced here: 73.3 us
  Pallas kernels  69 us (94%)
  local copies, waits for them, and re-layouts  3.06 us (4%)
  between operations  1.29 us (2%)
    pallas_call x1, Pallas kernels, per_device(): pl.pallas_call(functools.partial(kernel, sky_size, scale), out_shape=(jax...  69 us
    unnamed x4, local copies, waits for them, and re-layouts  3.06 us

profile of v6, /device:TPU:1, one launch (start us, length us, event | category | flops | bytes accessed | tf_op | source)
XLA Modules:
  0.0 73.3 jit_solution(9892656440345581232)
XLA Ops:
  1.3 0.8 %copy.11.chosen = s32[1,4,2]{2,1,0:T(4,128)S(1)} copy(s32[1,4,2]{1,2,0:T(2,128)} %param.15) | data formatting | bytes 64 | tf_op args[7]
  2.0 69.0 %shard_map.103 = (bf16[8,256,128]{2,1,0:T(8,128)(2,1)S(1)}, bf16[8,256,128]{2,1,0:T(8,128)(2,1)S(1)}, f32[4,128,128]{2,1,0:T(8,128)S(1)}) custom-call(bf16[8,256,128]{2,1,0:T(8,128)(2,1)} %bitcast.10, bf16[8,256,128]{2,1,0:T(8,128)(2,1)} %bitcast.11, bf16[4,128,128]{2,1,0:T(8,128)(2,1)} %filters_in.1, s32[24]{0:T(128)} %bitcast.12, s32[24]{0:T(128)} %bitcast.13, ...), custom_call_target="tpu_custom_call" | custom-call | flops 3221225472 | bytes 3145728 | tf_op jit(solution)/shard_map/pallas_call | solution.py:503
  71.0 0.8 %copy.16 = bf16[1,2048,128]{2,1,0:T(8,128)(2,1)} copy(bf16[1,2048,128]{2,1,0:T(8,128)(2,1)S(1)} %bitcast.8) | data formatting | bytes 1048576
  71.8 0.8 %copy.17 = bf16[1,2048,128]{2,1,0:T(8,128)(2,1)} copy(bf16[1,2048,128]{2,1,0:T(8,128)(2,1)S(1)} %bitcast.7) | data formatting | bytes 1048576
  72.6 0.7 copy.18
